TPU v7x, 256 devices: a whole 4x4x8 slice. The times are simulated.
256 devices in a mesh: grp: 16 (over x, y_lo, core), blk: 16 (over y_hi, z).
Axes of the slice: x: 4, y: 4 (y_hi: 2, y_lo: 2; y = y_hi * 2 + y_lo), z: 8, core: 2. Of those that a mesh axis runs over, the one named last changes fastest.
Arguments:
- member_embed: float32 [16, 4096, 768], P('grp', 'blk'), may hold values from -64 to 64
- sizes: int32 [16], replicated, may hold values from 1 to 4096, 32768 in all
- order: int32 [16, 4096], P('grp', 'blk'), may hold values from 0 to 4095, each once within a row
- ref_embed: float32 [16, 8192, 768], P(None, ('grp', 'blk')), may hold values from -64 to 64
Outputs:
- log_total: float32 [16, 4096], P('grp', 'blk')
- neighbour: bfloat16 [16, 4096, 768], P('grp', 'blk')
Inputs may be any that keep to these rules, and one draw needn't show every extreme that they name: Each cluster's row of order is a permutation of 0 to 4095.
All inputs are finite; a program needn't handle non-finite values.
Results may differ from a plain program's by a relative error of at most 0.0068.
Values may be sent and summed in bfloat16 or wider, within the bound.
A program may use at most 128 MiB of HBM per device.

v0:
```python
import jax
import jax.numpy as jnp
from jax import lax
from jax.sharding import PartitionSpec as P

SCALE = 32


def unit_rows(values):
    mean_square = jnp.mean(values * values, axis=-1, keepdims=True)
    return (values * lax.rsqrt(mean_square + 1e-06)).astype(jnp.bfloat16)


def per_device(member_embed, sizes, order, ref_embed):
    row_count = member_embed.shape[1]
    feature_width = member_embed.shape[2]
    queries = unit_rows(member_embed[0])
    ref_local = unit_rows(ref_embed)
    ref_rows = lax.all_to_all(ref_local, "grp", split_axis=0, concat_axis=1, tiled=True).reshape(
        -1, feature_width
    )
    cluster = lax.axis_index("grp")
    cluster_count = sizes.shape[0]
    live_count = jnp.sum(jnp.where(jnp.arange(cluster_count, dtype=jnp.int32) == cluster, sizes, 0))
    slot_index = lax.axis_index("blk") * row_count + jnp.arange(row_count, dtype=jnp.int32)
    live_rows = slot_index < live_count
    sentinel = lax.axis_size("blk") * row_count
    query_ranks = order[0]
    key_ranks = jnp.where(live_rows, query_ranks, sentinel)
    logit_scale = SCALE / feature_width
    key_rows = lax.all_gather(queries, "blk", axis=0, tiled=True)
    piece_ranks = lax.all_gather(key_ranks, "blk", axis=0, tiled=True)
    logits = lax.dot_general(
        queries, key_rows, (((1,), (1,)), ((), ())), preferred_element_type=jnp.float32
    )
    weight = jnp.where(
        piece_ranks[None, :] < query_ranks[:, None], jnp.exp(logits * logit_scale - SCALE), 0.0
    )
    summed = jnp.sum(weight, axis=1)
    mixed = jnp.dot(weight.astype(jnp.bfloat16), key_rows, preferred_element_type=jnp.float32)
    partial_value = (summed, mixed)
    key_rows = lax.all_gather(ref_rows, "blk", axis=0, tiled=True)
    logits = lax.dot_general(
        queries, key_rows, (((1,), (1,)), ((), ())), preferred_element_type=jnp.float32
    )
    weight = jnp.exp(logits * logit_scale - SCALE)
    summed = partial_value[0] + jnp.sum(weight, axis=1)
    mixed = partial_value[1] + jnp.dot(
        weight.astype(jnp.bfloat16), key_rows, preferred_element_type=jnp.float32
    )
    divisor = jnp.where(live_rows, summed, 1.0)
    log_values = jnp.where(live_rows, SCALE + jnp.log(divisor), 0.0)
    mean_rows = jnp.where(live_rows[:, None], mixed / divisor[:, None], 0.0).astype(jnp.bfloat16)
    return (log_values[None], mean_rows[None])


def solution(mesh):
    placed = (P("grp", "blk", None), P(), P("grp", "blk"), P(None, ("grp", "blk"), None))
    return jax.shard_map(
        per_device,
        mesh=mesh,
        in_specs=placed,
        out_specs=(P("grp", "blk"), P("grp", "blk", None)),
        check_vma=False,
    )
```

profile of v0, /device:TPU:4, one launch (start us, length us, event | category | flops | bytes accessed | tf_op | source)
XLA Modules:
  0.0 343.5 jit_solution(10847951838793169281)
XLA Ops:
  7.2 0.0 copy-start
  7.2 0.0 copy-start.4
  7.2 0.0 copy-start.2
  7.2 0.0 all-gather.4.cloned.1.call-start
  7.2 1.4 fusion.24
  8.6 2.0 fusion.25
  10.6 0.0 copy-start.1
  10.6 0.0 all-gather.4.cloned.1.call-update
  10.6 0.0 all-gather.6.cloned.1.call-start
  10.7 1.6 multiply_reduce_fusion
  12.3 0.0 copy-done
  12.3 0.1 multiply_convert_fusion
  12.5 16.8 %all_to_all.4 = bf16[16,32,768]{2,1,0:T(8,128)(2,1)} all-to-all(bf16[16,32,768]{2,1,0:T(8,128)(2,1)S(1)} %multiply_convert_fusion), channel_id=1, replica_groups=mesh['grp'=16,'blk'=16] {'grp'}, dimensions={0} | all-to-all | bytes 1572864 | tf_op jit(solution)/shard_map/all_to_all | solution.py:19
  29.3 0.0 all-gather.6.cloned.1.call-update
  29.3 0.0 copy-done.4
  29.4 0.6 fusion.27
  30.0 0.0 copy-done.2
  30.0 0.6 broadcast_select_fusion.1
  30.6 43.8 %all-gather = s32[16,1,256]{2,1,0:T(1,128)S(1)} all-gather(s32[1,1,256]{2,1,0:T(1,128)S(1)} %bitcast.24), channel_id=1, replica_groups=mesh['grp'=16,'blk'=16] {'blk'}, dimensions={0}, use_global_device_ids=true | all-gather | bytes 17408 | tf_op jit(solution)/shard_map/all_gather | solution.py:32
  74.3 57.1 %all-gather.4.cloned.1.call-done = bf16[4096,768]{1,0:T(8,128)(2,1)} async-done(((bf16[256,768]{1,0:T(8,128)(2,1)}), bf16[4096,768]{1,0:T(8,128)(2,1)}) %all-gather.4.cloned.1.call-update) | async-done | bytes 6291472 | tf_op jit(solution)/shard_map/all_gather | solution.py:31
  131.5 0.0 copy-done.1
  131.5 4.9 %fusion.28 = (f32[256]{0:T(256)S(1)}, bf16[256,4096]{1,0:T(8,128)(2,1)S(1)}) fusion(bf16[256,768]{1,0:T(8,128)(2,1)S(1)} %copy-done.1, bf16[4096,768]{1,0:T(8,128)(2,1)} %all-gather.4.cloned.1.call-done, s32[256]{0:T(256)S(1)} %bitcast.27, s32[4096]{0:T(1024)S(1)} %bitcast.23), kind=kOutput, calls=%fused_computation.33 | convolution fusion | flops 1616903936 | bytes 8800256 | tf_op jit(solution)/shard_map/dot_general | solution.py:33
  136.4 173.3 %all-gather.6.cloned.1.call-done = bf16[8192,768]{1,0:T(8,128)(2,1)} async-done(((bf16[512,768]{1,0:T(8,128)(2,1)}), bf16[8192,768]{1,0:T(8,128)(2,1)}) %all-gather.6.cloned.1.call-update) | async-done | bytes 12582928 | tf_op jit(solution)/shard_map/all_gather | solution.py:42
  309.6 14.3 %fusion.29 = (f32[256]{0:T(256)S(1)}, bf16[256,8192]{1,0:T(8,128)(2,1)}) fusion(bf16[256,768]{1,0:T(8,128)(2,1)S(1)} %copy-done.1, bf16[8192,768]{1,0:T(8,128)(2,1)} %all-gather.6.cloned.1.call-done), kind=kOutput, calls=%fused_computation.34 | convolution fusion | flops 3229613824 | bytes 17171456 | tf_op jit(solution)/shard_map/dot_general | solution.py:43
  323.9 1.1 compare_select_fusion
  325.0 0.0 copy-start.3
  325.0 9.0 %fusion.5 = f32[256,768]{1,0:T(8,128)S(1)} fusion(bf16[8192,768]{1,0:T(8,128)(2,1)} %all-gather.6.cloned.1.call-done, bf16[256,8192]{1,0:T(8,128)(2,1)} %get-tuple-element.9), kind=kOutput, calls=%fused_computation.7 | convolution fusion | flops 3221225472 | bytes 17563648 | tf_op jit(solution)/shard_map/dot_general | solution.py:48
  334.0 0.0 copy-done.3
  334.0 2.6 fusion.21
  (3 shorter events, 0.0 us)
Async XLA Ops:
  7.2 5.2 %copy-start = (f32[16,32,768]{2,1,0:T(8,128)S(1)}, f32[16,32,768]{2,1,0:T(8,128)}, u32[]{:S(2)}) copy-start(f32[16,32,768]{2,1,0:T(8,128)} %param.7) | copy-start | bytes 4718596
  7.2 22.2 %copy-start.4 = (s32[16]{0:T(128)S(1)}, s32[16]{0:T(128)}, u32[]{:S(2)}) copy-start(s32[16]{0:T(128)} %param.5) | copy-start | bytes 196
  7.2 22.8 %copy-start.2 = (s32[1,256]{1,0:T(1,128)S(1)}, s32[1,256]{1,0:T(1,128)}, u32[]{:S(2)}) copy-start(s32[1,256]{1,0:T(1,128)} %param.6) | copy-start | bytes 3076
  7.2 124.3 %all-gather.4.cloned.1.call-start = ((), (), s32[]{:S(2)}) async-start(), calls=%async_computation.1 | async-start | bytes 6684672 | tf_op jit(solution)/shard_map/all_gather | solution.py:31
  10.6 120.8 %copy-start.1 = (bf16[256,768]{1,0:T(8,128)(2,1)S(1)}, bf16[256,768]{1,0:T(8,128)(2,1)}, u32[]{:S(2)}) copy-start(bf16[256,768]{1,0:T(8,128)(2,1)} %fusion.25) | copy-start | bytes 1179652
  10.6 299.0 %all-gather.6.cloned.1.call-start = ((), (), s32[]{:S(2)}) async-start(), calls=%async_computation.2 | async-start | bytes 13369344 | tf_op jit(solution)/shard_map/all_gather | solution.py:42
  325.0 9.0 %copy-start.3 = (bf16[4096,768]{1,0:T(8,128)(2,1)S(1)}, bf16[4096,768]{1,0:T(8,128)(2,1)}, u32[]{:S(2)}) copy-start(bf16[4096,768]{1,0:T(8,128)(2,1)} %all-gather.4.cloned.1.call-done) | copy-start | bytes 18874372
Sparse Core Ops, SparseCore 0:
  11.2 120.2 all-gather.3
  134.0 175.5 all-gather.5
where the time goes:
time: 344 us; the launch traced here: 343 us
  waiting for transfers between devices  230 us (67%)
  blocking collectives  60.6 us (18%)
  matrix products  30.8 us (9%)
  between operations  14.1 us (4%)
  other arithmetic  7.51 us (2%)
    all_gather x1, waiting for transfers between devices, per_device(): key_rows = lax.all_gather(ref_rows, 'blk', axis=0, tiled=True)  173 us
    all_gather x1, waiting for transfers between devices, per_device(): key_rows = lax.all_gather(queries, 'blk', axis=0, tiled=True)  57.1 us
    all_gather x1, blocking collectives, per_device(): piece_ranks = lax.all_gather(key_ranks, 'blk', axis=0, tiled=True)  43.8 us
    dot_general x2, matrix products, per_device(): lax.dot_general(queries, key_rows, (((1,), (1,)), ((), ())), preferred_el...  19.2 us
    all_to_all x1, blocking collectives, per_device(): lax.all_to_all(ref_local, 'grp', split_axis=0, concat_axis=1, tiled=True)  16.8 us
    dot_general x2, matrix products, per_device(): jnp.dot(weight.astype(jnp.bfloat16), key_rows, preferred_element_type=jnp...  11.6 us
  transfers between devices with their start and end apart: 2, of which 2 were waited for; matrix products, arithmetic and copies ran while one was open for 2% of the time, Pallas kernels for 0%

commit v1 on v0

v1 whole, which is shorter than its diff:
```python
import functools
import math

import jax
import jax.numpy as jnp
from jax import lax
from jax.experimental import pallas as pl
from jax.experimental.pallas import tpu as pltpu
from jax.sharding import PartitionSpec as P

SCALE = 32
MESH = pl.DeviceIdType.MESH
LOG2E = math.log2(math.e)
STEPS = (0, 1, 7, 2, 6, 3, 5, 4)


def unit_rows(values):
    mean_square = jnp.mean(values * values, axis=-1, keepdims=True)
    return (values * lax.rsqrt(mean_square + 1e-06)).astype(jnp.bfloat16)


def device(x, y, z, core):
    return ((x * 2 + y % 2) * 2 + core, (y // 2) * 8 + z)


def lanes_to_rows(tile):
    wide = jnp.concatenate([tile] * 8, axis=0)
    row = lax.broadcasted_iota(jnp.int32, (64, 128), 0)
    lane = lax.broadcasted_iota(jnp.int32, (64, 128), 1)
    return jnp.sum(jnp.where(row == lane, wide, 0.0), axis=1, keepdims=True)


def rows_to_lanes(column):
    row = lax.broadcasted_iota(jnp.int32, (64, 128), 0)
    lane = lax.broadcasted_iota(jnp.int32, (64, 128), 1)
    spread = jnp.where(row == lane % 64, jnp.broadcast_to(column, (64, 128)), 0.0)
    return jnp.broadcast_to(jnp.sum(spread, axis=0, keepdims=True), (8, 128))


def slot_position(delta):
    return delta + delta // 2 - 2 * (delta // 3)


def kernel(
    member_hbm, sizes_ref, order_ref, ref_hbm, log_ref, mean_ref,
    member_in, ref_in, home_rows, home_rank, ref_unit, query, rank, key_member, rank_partner, ref_other, key_ref,
    part_sum, part_total, mix_send, mix_recv, tot_send, tot_recv, own_mix, own_tot,
    x_send, x_recv, xt_send, xt_recv, done_rows, done_log, home_log,
    load_sem, s_a, r_a, s_x, r_x, s_c, r_c, s_y, r_y, s_z, r_z, s_ry, r_ry,
    s_m, r_m, s_t, r_t, s_h, r_h,
):
    g = lax.axis_index("grp")
    b = lax.axis_index("blk")
    x, y, z, core = g // 4, (b // 8) * 2 + (g // 2) % 2, b % 8, g % 2
    parity = y % 2
    other = 1 - core
    home_z = 2 * x + core
    work_x, work_core = z // 2, z % 2
    is_self = home_z == z
    work_group = (work_x * 2 + parity) * 2 + work_core

    def source_z(position):
        return 2 * ((z // 2 + slot_position(position)) % 4) + core

    load_members = pltpu.make_async_copy(member_hbm.at[0], member_in, load_sem.at[0])
    load_refs = pltpu.make_async_copy(ref_hbm, ref_in, load_sem.at[1])
    load_members.start()
    load_refs.start()

    barrier = pltpu.get_barrier_semaphore()

    def greet(target):
        pl.semaphore_signal(barrier, inc=1, device_id=target, device_id_type=MESH)

    for step in (1, 2, 3):
        greet(device((x + step) % 4, y, z, core))
        greet(device(x, (y + step) % 4, z, core))
    for step in range(1, 8):
        greet(device(x, y, (z + step) % 8, core))
    greet(device(x, y, z, other))
    for position in range(4):
        from_z = source_z(position)

        @pl.when(jnp.logical_not(jnp.logical_and(is_self, from_z == z)))
        def _():
            greet(device(work_x, y, from_z, work_core))

    for quarter in range(4):

        @pl.when(jnp.logical_not(jnp.logical_and(is_self, x == quarter)))
        def _():
            greet(device(quarter, y, home_z, z % 2))

    load_members.wait()
    home_rows[...] = unit_rows(member_in[...])
    live_count = sizes_ref[g]
    slot = lax.broadcasted_iota(jnp.int32, (1, 256), 1) + b * 256
    ranks = jnp.where(slot < live_count, order_ref[...], 4096).astype(jnp.float32)
    for quarter in range(4):
        piece = ranks[:, 64 * quarter : 64 * quarter + 64]
        home_rank[quarter] = jnp.broadcast_to(jnp.concatenate([piece, piece], axis=1), (8, 128))

    pl.semaphore_wait(barrier, 22 - 2 * is_self.astype(jnp.int32))

    sent = []

    def send(src, dst, send_sem, recv_sem, target):
        copy = pltpu.make_async_remote_copy(
            src_ref=src, dst_ref=dst, send_sem=send_sem, recv_sem=recv_sem, device_id=target, device_id_type=MESH
        )
        copy.start()
        sent.append(copy)
        return copy

    def landed(dst, sem):
        pltpu.make_async_copy(dst, dst, sem).wait()

    here = slot_position((z // 2 - home_z // 2 + 4) % 4)
    row_owner = z % 2 * 4
    first = []
    for quarter in range(4):
        pairs = (
            (home_rows.at[pl.ds(64 * quarter, 64)], query.at[here, row_owner + quarter], 0),
            (home_rank.at[quarter], rank.at[here, row_owner + quarter], 1),
        )
        target = device(quarter, y, home_z, z % 2)
        mine = jnp.logical_and(is_self, x == quarter)
        for src, dst, kind in pairs:
            remote = pltpu.make_async_remote_copy(
                src_ref=src, dst_ref=dst, send_sem=s_a.at[kind, quarter], recv_sem=r_a.at[kind, here],
                device_id=target, device_id_type=MESH,
            )
            local = pltpu.make_async_copy(src, dst, r_a.at[kind, here])
            first.append((mine, remote))

            @pl.when(mine)
            def _():
                local.start()

            @pl.when(jnp.logical_not(mine))
            def _():
                remote.start()

    load_refs.wait()
    for group in range(4):
        ref_unit[pl.ds(4 * group, 4)] = unit_rows(ref_in[pl.ds(4 * group, 4)])

    def ref_index(to_z, side):
        return (to_z // 2) * 4 + side * 2 + to_z % 2

    key_ref[0, 0] = ref_unit[ref_index(z, parity)]
    ref_other[0] = ref_unit[ref_index(z, 1 - parity)]
    for i in range(1, 8):
        to_z = (z + 8 - STEPS[i]) % 8
        target = device(x, y, to_z, core)
        send(ref_unit.at[ref_index(to_z, parity)], key_ref.at[i, 0], s_z.at[0, i], r_z.at[0, i], target)
        send(ref_unit.at[ref_index(to_z, 1 - parity)], ref_other.at[i], s_z.at[1, i], r_z.at[1, i], target)

    opposite = device(x, (y + 2) % 4, z, core)
    above = device(x, (y + 1) % 4, z, core)
    below = device(x, (y + 3) % 4, z, core)

    def pass_refs(i):
        if i:
            landed(key_ref.at[i, 0], r_z.at[0, i])
            landed(ref_other.at[i], r_z.at[1, i])
        send(key_ref.at[i, 0], key_ref.at[i, 1], s_ry.at[0, i], r_ry.at[0, i], opposite)
        send(ref_other.at[i], key_ref.at[i, 2], s_ry.at[1, i], r_ry.at[1, i], above)
        send(ref_other.at[i], key_ref.at[i, 3], s_ry.at[2, i], r_ry.at[2, i], below)

    pass_refs(0)

    me = core * 4 + x

    def pass_queries(t):
        landed(query.at[t, me], r_a.at[0, t])
        landed(rank.at[t, me], r_a.at[1, t])
        for step in (2, 1, 3):
            target = device((x + step) % 4, y, z, core)
            send(query.at[t, me], query.at[t, me], s_x.at[0, step - 1, t], r_x.at[0, step - 1, t], target)
            send(rank.at[t, me], rank.at[t, me], s_x.at[1, step - 1, t], r_x.at[1, step - 1, t], target)
        send(query.at[t, me], key_member.at[1, t], s_y.at[0, t], r_y.at[0, t], opposite)
        send(rank.at[t, me], rank_partner.at[t], s_y.at[1, t], r_y.at[1, t], opposite)
        key_member[0, t] = query[t, me]

    sibling = device(x, y, z, other)
    my_half, other_half = pl.ds(core * 4, 4), pl.ds(other * 4, 4)

    def share_queries(t):
        for step in (1, 3, 2):
            from_x = core * 4 + (x + 4 - step) % 4
            landed(query.at[t, from_x], r_x.at[0, step - 1, t])
            landed(rank.at[t, from_x], r_x.at[1, step - 1, t])
        send(query.at[t, my_half], query.at[t, my_half], s_c.at[0, t], r_c.at[0, t], sibling)
        send(rank.at[t, my_half], rank.at[t, my_half], s_c.at[1, t], r_c.at[1, t], sibling)

    for t in range(4):
        pass_queries(t)
    pass_refs(1)
    pass_refs(2)
    share_queries(0)
    pass_refs(3)
    pass_refs(4)
    share_queries(1)
    pass_refs(5)
    pass_refs(6)
    share_queries(2)
    pass_refs(7)
    share_queries(3)

    for t in range(4):
        landed(key_member.at[1, t], r_y.at[0, t])
        landed(rank_partner.at[t], r_y.at[1, t])
        landed(query.at[t, other_half], r_c.at[0, t])
        landed(rank.at[t, other_half], r_c.at[1, t])
    for i in range(8):
        for side in range(3):
            landed(key_ref.at[i, side + 1], r_ry.at[side, i])

    low = lax.broadcasted_iota(jnp.int32, (8, 128), 1) < 64
    key_rank = jnp.concatenate(
        [
            jnp.where(low, rank[0, me], rank[1, me]),
            jnp.where(low, rank[2, me], rank[3, me]),
            jnp.where(low, rank_partner[0], rank_partner[1]),
            jnp.where(low, rank_partner[2], rank_partner[3]),
        ],
        axis=1,
    )[0:1]

    def weigh(rows, keys):
        logits = lax.dot_general(rows, keys, (((1,), (1,)), ((), ())), preferred_element_type=jnp.float32)
        return jnp.exp2(logits * (SCALE / 768 * LOG2E) - SCALE * LOG2E)

    def compute(t):
        rows = query[t].reshape(512, 768)
        row_rank = jnp.concatenate([lanes_to_rows(rank[t, owner]) for owner in range(8)], axis=0)
        keys = key_member[...].reshape(512, 768)
        weight = jnp.where(key_rank < row_rank, weigh(rows, keys), 0.0)
        total = jnp.sum(weight, axis=1, keepdims=True)
        mixed = jnp.dot(weight.astype(jnp.bfloat16), keys, preferred_element_type=jnp.float32)
        for half in range(2):
            keys = key_ref[pl.ds(4 * half, 4)].reshape(512, 768)
            weight = weigh(rows, keys)
            total = total + jnp.sum(weight, axis=1, keepdims=True)
            mixed = mixed + jnp.dot(weight.astype(jnp.bfloat16), keys, preferred_element_type=jnp.float32)
        part_sum[t] = mixed.reshape(8, 64, 768)
        for owner in range(8):
            part_total[t, owner] = rows_to_lanes(total[64 * owner : 64 * owner + 64])
        mix_send[t] = part_sum[t, other_half].astype(jnp.bfloat16)
        tot_send[t] = part_total[t, other_half]
        send(mix_send.at[t], mix_recv.at[t], s_m.at[0, t], r_m.at[0, t], sibling)
        send(tot_send.at[t], tot_recv.at[t], s_m.at[1, t], r_m.at[1, t], sibling)

    def to_owner(t):
        landed(mix_recv.at[t], r_m.at[0, t])
        landed(tot_recv.at[t], r_m.at[1, t])
        mixed = part_sum[t, my_half] + mix_recv[t].astype(jnp.float32)
        total = part_total[t, my_half] + tot_recv[t]
        part_sum[t, my_half] = mixed
        part_total[t, my_half] = total
        x_send[t] = mixed.astype(jnp.bfloat16)
        xt_send[t] = total
        for step in (2, 1, 3):
            to_x = (x + step) % 4
            target = device(to_x, y, z, core)
            send(x_send.at[t, to_x], x_recv.at[t, step - 1], s_t.at[0, step - 1, t], r_t.at[0, step - 1, t], target)
            send(xt_send.at[t, to_x], xt_recv.at[t, step - 1], s_t.at[1, step - 1, t], r_t.at[1, step - 1, t], target)

    last = []

    def finish(t):
        mixed = part_sum[t, me]
        total = part_total[t, me]
        for step in (1, 3, 2):
            landed(x_recv.at[t, step - 1], r_t.at[0, step - 1, t])
            landed(xt_recv.at[t, step - 1], r_t.at[1, step - 1, t])
            mixed = mixed + x_recv[t, step - 1].astype(jnp.float32)
            total = total + xt_recv[t, step - 1]
        from_z = source_z(t)
        start = (y // 2 * 8 + from_z) * 256 + 64 * x
        count = sizes_ref[work_group]
        slot_lane = lax.broadcasted_iota(jnp.int32, (8, 128), 1) % 64 + start
        divisor = jnp.where(slot_lane < count, total, 1.0)
        done_log[t] = jnp.where(slot_lane < count, SCALE + jnp.log(divisor), 0.0)
        slot_row = lax.broadcasted_iota(jnp.int32, (64, 1), 0) + start
        mean = jnp.where(slot_row < count, mixed / lanes_to_rows(divisor), 0.0)
        done_rows[t] = mean.astype(jnp.bfloat16)
        target = device(work_x, y, from_z, work_core)
        mine = jnp.logical_and(is_self, from_z == z)
        pairs = ((done_rows.at[t], mean_ref.at[0, pl.ds(pl.multiple_of(64 * x, 64), 64)], 0), (done_log.at[t], home_log.at[x], 1))
        for src, dst, kind in pairs:
            remote = pltpu.make_async_remote_copy(
                src_ref=src, dst_ref=dst, send_sem=s_h.at[kind, t], recv_sem=r_h.at[kind, x],
                device_id=target, device_id_type=MESH,
            )
            local = pltpu.make_async_copy(src, dst, r_h.at[kind, x])
            last.append((mine, remote))

            @pl.when(mine)
            def _():
                local.start()

            @pl.when(jnp.logical_not(mine))
            def _():
                remote.start()

    for t in range(6):
        if t < 4:
            compute(t)
        if 1 <= t < 5:
            to_owner(t - 1)
        if t >= 2:
            finish(t - 2)

    for quarter in range(4):
        landed(mean_ref.at[0, pl.ds(64 * quarter, 64)], r_h.at[0, quarter])
        landed(home_log.at[quarter], r_h.at[1, quarter])
    log_ref[...] = jnp.concatenate(
        [jnp.where(low, home_log[0], home_log[1])[0:1], jnp.where(low, home_log[2], home_log[3])[0:1]], axis=1
    )
    for copy in sent:
        copy.wait_send()
    for mine, remote in first + last:

        @pl.when(jnp.logical_not(mine))
        def _():
            remote.wait_send()


def per_device(member_embed, sizes, order, ref_embed):
    vmem = pl.BlockSpec(memory_space=pltpu.VMEM)
    anywhere = pl.BlockSpec(memory_space=pl.ANY)
    bf16, f32 = jnp.bfloat16, jnp.float32
    dma = pltpu.SemaphoreType.DMA
    return pl.pallas_call(
        kernel,
        out_shape=(jax.ShapeDtypeStruct((1, 256), f32), jax.ShapeDtypeStruct((1, 256, 768), bf16)),
        in_specs=[anywhere, pl.BlockSpec(memory_space=pltpu.SMEM), vmem, anywhere],
        out_specs=(vmem, vmem),
        scratch_shapes=[
            pltpu.VMEM((256, 768), f32),
            pltpu.VMEM((16, 32, 768), f32),
            pltpu.VMEM((256, 768), bf16),
            pltpu.VMEM((4, 8, 128), f32),
            pltpu.VMEM((16, 32, 768), bf16),
            pltpu.VMEM((4, 8, 64, 768), bf16),
            pltpu.VMEM((4, 8, 8, 128), f32),
            pltpu.VMEM((2, 4, 64, 768), bf16),
            pltpu.VMEM((4, 8, 128), f32),
            pltpu.VMEM((8, 32, 768), bf16),
            pltpu.VMEM((8, 4, 32, 768), bf16),
            pltpu.VMEM((4, 8, 64, 768), f32),
            pltpu.VMEM((4, 8, 8, 128), f32),
            pltpu.VMEM((4, 4, 64, 768), bf16),
            pltpu.VMEM((4, 4, 64, 768), bf16),
            pltpu.VMEM((4, 4, 8, 128), f32),
            pltpu.VMEM((4, 4, 8, 128), f32),
            pltpu.VMEM((8, 128), f32),
            pltpu.VMEM((8, 128), f32),
            pltpu.VMEM((4, 4, 64, 768), bf16),
            pltpu.VMEM((4, 3, 64, 768), bf16),
            pltpu.VMEM((4, 4, 8, 128), f32),
            pltpu.VMEM((4, 3, 8, 128), f32),
            pltpu.VMEM((4, 64, 768), bf16),
            pltpu.VMEM((4, 8, 128), f32),
            pltpu.VMEM((4, 8, 128), f32),
            dma((2,)),
            dma((2, 4)), dma((2, 4)),
            dma((2, 3, 4)), dma((2, 3, 4)),
            dma((2, 4)), dma((2, 4)),
            dma((2, 4)), dma((2, 4)),
            dma((2, 8)), dma((2, 8)),
            dma((3, 8)), dma((3, 8)),
            dma((2, 4)), dma((2, 4)),
            dma((2, 3, 4)), dma((2, 3, 4)),
            dma((2, 4)), dma((2, 4)),
        ],
        compiler_params=pltpu.CompilerParams(
            collective_id=0, has_side_effects=True, vmem_limit_bytes=56 * 1024 * 1024
        ),
        cost_estimate=pl.CostEstimate(flops=4 * 2048 * 1536 * 768, bytes_accessed=4 << 20, transcendentals=2048 * 1536),
        name="dedup_scores",
    )(member_embed, sizes, order, ref_embed)


def solution(mesh):
    placed = (P("grp", "blk", None), P(), P("grp", "blk"), P(None, ("grp", "blk"), None))
    return jax.shard_map(
        per_device,
        mesh=mesh,
        in_specs=placed,
        out_specs=(P("grp", "blk"), P("grp", "blk", None)),
        check_vma=False,
    )
```

time: 344 us -> 118 us (0.34)
  waiting for transfers between devices: 230 us -> 0 us
  Pallas kernels: 0 us -> 114 us
  blocking collectives: 60.6 us -> 0 us
  matrix products: 30.8 us -> 0 us
  between operations: 14.1 us -> 0.64 us
  other arithmetic: 7.51 us -> 0 us
    all_gather x2 -> x0, waiting for transfers between devices: 230 us -> none  [the longest x1 173 us: per_device(): key_rows = lax.all_gather(ref_rows, 'blk', axis=0, tiled=True)]
    pallas_call x0 -> x1, Pallas kernels: none -> 114 us  [per_device(): pl.pallas_call(kernel, out_shape=(jax.ShapeDtypeStruct((1, 256), f32), ja...]
    all_gather x1 -> x0, blocking collectives: 43.8 us -> none  [per_device(): piece_ranks = lax.all_gather(key_ranks, 'blk', axis=0, tiled=True)]
    dot_general x4 -> x0, matrix products: 30.8 us -> none  [the longest x2 19.2 us: per_device(): lax.dot_general(queries, key_rows, (((1,), (1,)), ((), ())), preferred_el...]
    all_to_all x1 -> x0, blocking collectives: 16.8 us -> none  [per_device(): lax.all_to_all(ref_local, 'grp', split_axis=0, concat_axis=1, tiled=True)]
    reduce_sum x3 -> x0, other arithmetic: 3.62 us -> none  [the longest x2 2.99 us: unit_rows(): mean_square = jnp.mean(values * values, axis=-1, keepdims=True)]
  transfers between devices with their start and end apart: 2 -> 0, of which waited for: 2 -> 0; matrix products, arithmetic and copies ran while one was open for 2% -> 0% of each run, Pallas kernels for 0% -> 0%
where the time goes in v1:
time: 118 us; the launch traced here: 117 us
  Pallas kernels  114 us (97%)
  local copies, waits for them, and re-layouts  2.96 us (3%)
    pallas_call x1, Pallas kernels, per_device(): pl.pallas_call(kernel, out_shape=(jax.ShapeDtypeStruct((1, 256), f32), ja...  114 us
    unnamed x2, local copies, waits for them, and re-layouts  2.96 us

profile of v1, /device:TPU:4, one launch (start us, length us, event | category | flops | bytes accessed | tf_op | source)
XLA Modules:
  0.0 117.3 jit_solution(12909164973446030356)
XLA Ops:
  0.6 113.8 %dedup_scores.1 = (f32[1,256]{1,0:T(1,128)}, bf16[1,256,768]{2,1,0:T(8,128)(2,1)}) custom-call(f32[1,256,768]{2,1,0:T(8,128)} %member_hbm.1, s32[16]{0:T(128)} %sizes_ref.1, s32[1,256]{1,0:T(1,128)} %order_ref.1, f32[16,32,768]{2,1,0:T(8,128)} %ref_hbm.1), custom_call_target="tpu_custom_call" | custom-call | flops 9663676416 | bytes 4194304 | tf_op jit(solution)/shard_map/dedup_scores/pallas_call | solution.py:336
  114.4 1.2 %copy.8 = f32[1,256]{1,0:T(1,128)} copy(f32[1,256]{1,0:T(1,128)} %get-tuple-element.4) | data formatting | bytes 2048
  115.6 1.8 %copy.9 = bf16[1,256,768]{2,1,0:T(8,128)(2,1)} copy(bf16[1,256,768]{2,1,0:T(8,128)(2,1)} %get-tuple-element.5) | data formatting | bytes 786432

commit v2 on v1

--- a/solution.py
+++ b/solution.py
@@ -11,7 +11,7 @@
 SCALE = 32
 MESH = pl.DeviceIdType.MESH
 LOG2E = math.log2(math.e)
-STEPS = (0, 1, 7, 2, 6, 3, 5, 4)
+STEPS = (0, 4, 1, 7, 2, 6, 3, 5)
 
 
 def unit_rows(values):
@@ -43,10 +43,10 @@
 
 def kernel(
     member_hbm, sizes_ref, order_ref, ref_hbm, log_ref, mean_ref,
-    member_in, ref_in, home_rows, home_rank, ref_unit, query, rank, key_member, rank_partner, ref_other, key_ref,
-    part_sum, part_total, mix_send, mix_recv, tot_send, tot_recv, own_mix, own_tot,
+    member_in, ref_in, home_rows, home_rank, hop_rows, hop_rank, ref_unit, query, rank, key_member, rank_partner, ref_other, key_ref,
+    part_sum, part_total, lane_total, mix_send, mix_recv, tot_send, tot_recv, own_mix, own_tot,
     x_send, x_recv, xt_send, xt_recv, done_rows, done_log, home_log,
-    load_sem, s_a, r_a, s_x, r_x, s_c, r_c, s_y, r_y, s_z, r_z, s_ry, r_ry,
+    load_sem, s_q, r_q, s_a, r_a, s_x, r_x, s_c, r_c, s_y, r_y, s_z, r_z, s_ry, r_ry,
     s_m, r_m, s_t, r_t, s_h, r_h,
 ):
     g = lax.axis_index("grp")
@@ -57,7 +57,11 @@
     home_z = 2 * x + core
     work_x, work_core = z // 2, z % 2
     is_self = home_z == z
+    stays = z % 2 == core
     work_group = (work_x * 2 + parity) * 2 + work_core
+
+    z_steps = [(step + core * (8 - 2 * step)) % 8 for step in STEPS]
+    x_steps = [step + core * (4 - 2 * step) for step in (2, 1, 3)]
 
     def source_z(position):
         return 2 * ((z // 2 + slot_position(position)) % 4) + core
@@ -81,9 +85,9 @@
     for position in range(4):
         from_z = source_z(position)
 
-        @pl.when(jnp.logical_not(jnp.logical_and(is_self, from_z == z)))
+        @pl.when(jnp.logical_not(jnp.logical_and(stays, from_z == z)))
         def _():
-            greet(device(work_x, y, from_z, work_core))
+            greet(device(x, y, from_z, z % 2))
 
     for quarter in range(4):
 
@@ -100,7 +104,11 @@
         piece = ranks[:, 64 * quarter : 64 * quarter + 64]
         home_rank[quarter] = jnp.broadcast_to(jnp.concatenate([piece, piece], axis=1), (8, 128))
 
-    pl.semaphore_wait(barrier, 22 - 2 * is_self.astype(jnp.int32))
+    load_refs.wait()
+    for group in range(4):
+        ref_unit[pl.ds(4 * group, 4)] = unit_rows(ref_in[pl.ds(4 * group, 4)])
+
+    pl.semaphore_wait(barrier, 22 - is_self.astype(jnp.int32) - stays.astype(jnp.int32))
 
     sent = []
 
@@ -115,20 +123,31 @@
     def landed(dst, sem):
         pltpu.make_async_copy(dst, dst, sem).wait()
 
-    here = slot_position((z // 2 - home_z // 2 + 4) % 4)
-    row_owner = z % 2 * 4
+    for i, step in enumerate(x_steps):
+        to_x = (x + step) % 4
+        target = device(to_x, y, z, core)
+        quarter = pl.ds(pl.multiple_of(64 * to_x, 64), 64)
+        send(home_rows.at[quarter], hop_rows.at[i], s_q.at[0, i], r_q.at[0, i], target)
+        send(home_rank.at[to_x], hop_rank.at[i], s_q.at[1, i], r_q.at[1, i], target)
+
+    row_owner = z % 2 * 4 + x
     first = []
-    for quarter in range(4):
-        pairs = (
-            (home_rows.at[pl.ds(64 * quarter, 64)], query.at[here, row_owner + quarter], 0),
-            (home_rank.at[quarter], rank.at[here, row_owner + quarter], 1),
-        )
-        target = device(quarter, y, home_z, z % 2)
-        mine = jnp.logical_and(is_self, x == quarter)
-        for src, dst, kind in pairs:
+
+    def to_row(i):
+        from_x = (x + 4 - x_steps[i]) % 4 if i < 3 else x
+        to_z = 2 * from_x + core
+        here = slot_position((z // 2 - from_x + 4) % 4)
+        if i < 3:
+            rows, ranks = hop_rows.at[i], hop_rank.at[i]
+            landed(rows, r_q.at[0, i])
+            landed(ranks, r_q.at[1, i])
+        else:
+            rows, ranks = home_rows.at[pl.ds(pl.multiple_of(64 * x, 64), 64)], home_rank.at[x]
+        mine = to_z == z
+        for src, dst, kind in ((rows, query.at[here, row_owner], 0), (ranks, rank.at[here, row_owner], 1)):
             remote = pltpu.make_async_remote_copy(
-                src_ref=src, dst_ref=dst, send_sem=s_a.at[kind, quarter], recv_sem=r_a.at[kind, here],
-                device_id=target, device_id_type=MESH,
+                src_ref=src, dst_ref=dst, send_sem=s_a.at[kind, i], recv_sem=r_a.at[kind, here],
+                device_id=device(x, y, to_z, z % 2), device_id_type=MESH,
             )
             local = pltpu.make_async_copy(src, dst, r_a.at[kind, here])
             first.append((mine, remote))
@@ -141,17 +160,13 @@
             def _():
                 remote.start()
 
-    load_refs.wait()
-    for group in range(4):
-        ref_unit[pl.ds(4 * group, 4)] = unit_rows(ref_in[pl.ds(4 * group, 4)])
-
     def ref_index(to_z, side):
         return (to_z // 2) * 4 + side * 2 + to_z % 2
 
     key_ref[0, 0] = ref_unit[ref_index(z, parity)]
     ref_other[0] = ref_unit[ref_index(z, 1 - parity)]
-    for i in range(1, 8):
-        to_z = (z + 8 - STEPS[i]) % 8
+    def send_refs(i):
+        to_z = (z + 8 - z_steps[i]) % 8
         target = device(x, y, to_z, core)
         send(ref_unit.at[ref_index(to_z, parity)], key_ref.at[i, 0], s_z.at[0, i], r_z.at[0, i], target)
         send(ref_unit.at[ref_index(to_z, 1 - parity)], ref_other.at[i], s_z.at[1, i], r_z.at[1, i], target)
@@ -168,17 +183,15 @@
         send(ref_other.at[i], key_ref.at[i, 2], s_ry.at[1, i], r_ry.at[1, i], above)
         send(ref_other.at[i], key_ref.at[i, 3], s_ry.at[2, i], r_ry.at[2, i], below)
 
-    pass_refs(0)
-
     me = core * 4 + x
 
     def pass_queries(t):
         landed(query.at[t, me], r_a.at[0, t])
         landed(rank.at[t, me], r_a.at[1, t])
-        for step in (2, 1, 3):
+        for i, step in enumerate(x_steps):
             target = device((x + step) % 4, y, z, core)
-            send(query.at[t, me], query.at[t, me], s_x.at[0, step - 1, t], r_x.at[0, step - 1, t], target)
-            send(rank.at[t, me], rank.at[t, me], s_x.at[1, step - 1, t], r_x.at[1, step - 1, t], target)
+            send(query.at[t, me], query.at[t, me], s_x.at[0, i, t], r_x.at[0, i, t], target)
+            send(rank.at[t, me], rank.at[t, me], s_x.at[1, i, t], r_x.at[1, i, t], target)
         send(query.at[t, me], key_member.at[1, t], s_y.at[0, t], r_y.at[0, t], opposite)
         send(rank.at[t, me], rank_partner.at[t], s_y.at[1, t], r_y.at[1, t], opposite)
         key_member[0, t] = query[t, me]
@@ -187,64 +200,72 @@
     my_half, other_half = pl.ds(core * 4, 4), pl.ds(other * 4, 4)
 
     def share_queries(t):
-        for step in (1, 3, 2):
-            from_x = core * 4 + (x + 4 - step) % 4
-            landed(query.at[t, from_x], r_x.at[0, step - 1, t])
-            landed(rank.at[t, from_x], r_x.at[1, step - 1, t])
+        for i in (1, 2, 0):
+            from_x = core * 4 + (x + 4 - x_steps[i]) % 4
+            landed(query.at[t, from_x], r_x.at[0, i, t])
+            landed(rank.at[t, from_x], r_x.at[1, i, t])
         send(query.at[t, my_half], query.at[t, my_half], s_c.at[0, t], r_c.at[0, t], sibling)
         send(rank.at[t, my_half], rank.at[t, my_half], s_c.at[1, t], r_c.at[1, t], sibling)
 
-    for t in range(4):
-        pass_queries(t)
-    pass_refs(1)
-    pass_refs(2)
-    share_queries(0)
-    pass_refs(3)
-    pass_refs(4)
-    share_queries(1)
-    pass_refs(5)
-    pass_refs(6)
-    share_queries(2)
-    pass_refs(7)
-    share_queries(3)
-
-    for t in range(4):
-        landed(key_member.at[1, t], r_y.at[0, t])
-        landed(rank_partner.at[t], r_y.at[1, t])
+    low = lax.broadcasted_iota(jnp.int32, (8, 128), 1) < 64
+
+    def queries_landed(t):
         landed(query.at[t, other_half], r_c.at[0, t])
         landed(rank.at[t, other_half], r_c.at[1, t])
-    for i in range(8):
-        for side in range(3):
-            landed(key_ref.at[i, side + 1], r_ry.at[side, i])
-
-    low = lax.broadcasted_iota(jnp.int32, (8, 128), 1) < 64
-    key_rank = jnp.concatenate(
-        [
-            jnp.where(low, rank[0, me], rank[1, me]),
-            jnp.where(low, rank[2, me], rank[3, me]),
-            jnp.where(low, rank_partner[0], rank_partner[1]),
-            jnp.where(low, rank_partner[2], rank_partner[3]),
-        ],
-        axis=1,
-    )[0:1]
-
-    def weigh(rows, keys):
-        logits = lax.dot_general(rows, keys, (((1,), (1,)), ((), ())), preferred_element_type=jnp.float32)
+
+    def members_landed():
+        for t in range(4):
+            landed(key_member.at[1, t], r_y.at[0, t])
+            landed(rank_partner.at[t], r_y.at[1, t])
+
+    def refs_landed(half):
+        for i in range(4 * half, 4 * half + 4):
+            for side in range(3):
+                landed(key_ref.at[i, side + 1], r_ry.at[side, i])
+
+    def weigh(t, keys):
+        logits = lax.dot_general(
+            query[t].reshape(512, 768), keys, (((1,), (1,)), ((), ())), preferred_element_type=jnp.float32
+        )
         return jnp.exp2(logits * (SCALE / 768 * LOG2E) - SCALE * LOG2E)
 
-    def compute(t):
-        rows = query[t].reshape(512, 768)
+    def lane_sums(weight):
+        return weight[:, 0:128] + weight[:, 128:256] + weight[:, 256:384] + weight[:, 384:512]
+
+    begun = set()
+
+    def add_up(t, weight, keys):
+        mixed = jnp.dot(weight.astype(jnp.bfloat16), keys, preferred_element_type=jnp.float32).reshape(8, 64, 768)
+        if t in begun:
+            lane_total[t] += lane_sums(weight)
+            part_sum[t] += mixed
+        else:
+            lane_total[t] = lane_sums(weight)
+            part_sum[t] = mixed
+            begun.add(t)
+
+    def compute_members(t):
+        key_rank = jnp.concatenate(
+            [
+                jnp.where(low, rank[0, me], rank[1, me]),
+                jnp.where(low, rank[2, me], rank[3, me]),
+                jnp.where(low, rank_partner[0], rank_partner[1]),
+                jnp.where(low, rank_partner[2], rank_partner[3]),
+            ],
+            axis=1,
+        )[0:1]
         row_rank = jnp.concatenate([lanes_to_rows(rank[t, owner]) for owner in range(8)], axis=0)
         keys = key_member[...].reshape(512, 768)
-        weight = jnp.where(key_rank < row_rank, weigh(rows, keys), 0.0)
-        total = jnp.sum(weight, axis=1, keepdims=True)
-        mixed = jnp.dot(weight.astype(jnp.bfloat16), keys, preferred_element_type=jnp.float32)
-        for half in range(2):
-            keys = key_ref[pl.ds(4 * half, 4)].reshape(512, 768)
-            weight = weigh(rows, keys)
-            total = total + jnp.sum(weight, axis=1, keepdims=True)
-            mixed = mixed + jnp.dot(weight.astype(jnp.bfloat16), keys, preferred_element_type=jnp.float32)
-        part_sum[t] = mixed.reshape(8, 64, 768)
+        weight = jnp.where(key_rank < row_rank, weigh(t, keys), 0.0)
+        add_up(t, weight, keys)
+
+    def compute_refs(t, half):
+        keys = key_ref[pl.ds(4 * half, 4)].reshape(512, 768)
+        weight = weigh(t, keys)
+        add_up(t, weight, keys)
+
+    def to_sibling(t):
+        total = jnp.sum(lane_total[t], axis=1, keepdims=True)
         for owner in range(8):
             part_total[t, owner] = rows_to_lanes(total[64 * owner : 64 * owner + 64])
         mix_send[t] = part_sum[t, other_half].astype(jnp.bfloat16)
@@ -261,22 +282,22 @@
         part_total[t, my_half] = total
         x_send[t] = mixed.astype(jnp.bfloat16)
         xt_send[t] = total
-        for step in (2, 1, 3):
+        for i, step in enumerate(x_steps):
             to_x = (x + step) % 4
             target = device(to_x, y, z, core)
-            send(x_send.at[t, to_x], x_recv.at[t, step - 1], s_t.at[0, step - 1, t], r_t.at[0, step - 1, t], target)
-            send(xt_send.at[t, to_x], xt_recv.at[t, step - 1], s_t.at[1, step - 1, t], r_t.at[1, step - 1, t], target)
+            send(x_send.at[t, to_x], x_recv.at[t, i], s_t.at[0, i, t], r_t.at[0, i, t], target)
+            send(xt_send.at[t, to_x], xt_recv.at[t, i], s_t.at[1, i, t], r_t.at[1, i, t], target)
 
     last = []
 
     def finish(t):
         mixed = part_sum[t, me]
         total = part_total[t, me]
-        for step in (1, 3, 2):
-            landed(x_recv.at[t, step - 1], r_t.at[0, step - 1, t])
-            landed(xt_recv.at[t, step - 1], r_t.at[1, step - 1, t])
-            mixed = mixed + x_recv[t, step - 1].astype(jnp.float32)
-            total = total + xt_recv[t, step - 1]
+        for i in (1, 2, 0):
+            landed(x_recv.at[t, i], r_t.at[0, i, t])
+            landed(xt_recv.at[t, i], r_t.at[1, i, t])
+            mixed = mixed + x_recv[t, i].astype(jnp.float32)
+            total = total + xt_recv[t, i]
         from_z = source_z(t)
         start = (y // 2 * 8 + from_z) * 256 + 64 * x
         count = sizes_ref[work_group]
@@ -305,13 +326,64 @@
             def _():
                 remote.start()
 
-    for t in range(6):
-        if t < 4:
-            compute(t)
-        if 1 <= t < 5:
-            to_owner(t - 1)
-        if t >= 2:
-            finish(t - 2)
+    send_refs(1)
+    pass_refs(0)
+    to_row(3)
+    to_row(1)
+    to_row(2)
+    to_row(0)
+    send_refs(2)
+    send_refs(3)
+    send_refs(4)
+    send_refs(5)
+    send_refs(6)
+    send_refs(7)
+    pass_queries(0)
+    pass_refs(1)
+    pass_queries(1)
+    pass_queries(2)
+    pass_refs(2)
+    pass_refs(3)
+    share_queries(0)
+    pass_queries(3)
+    pass_refs(4)
+    pass_refs(5)
+    share_queries(1)
+    share_queries(2)
+    queries_landed(0)
+    refs_landed(0)
+    compute_refs(0, 0)
+    queries_landed(1)
+    compute_refs(1, 0)
+    pass_refs(6)
+    queries_landed(2)
+    compute_refs(2, 0)
+    pass_refs(7)
+    share_queries(3)
+    members_landed()
+    compute_members(0)
+    compute_members(1)
+    compute_members(2)
+    queries_landed(3)
+    compute_refs(3, 0)
+    compute_members(3)
+    refs_landed(1)
+    compute_refs(0, 1)
+    to_sibling(0)
+    compute_refs(1, 1)
+    to_sibling(1)
+    to_owner(0)
+    compute_refs(2, 1)
+    to_sibling(2)
+    to_owner(1)
+    compute_refs(3, 1)
+    to_sibling(3)
+    to_owner(2)
+    to_owner(3)
+    finish(0)
+    finish(1)
+    finish(2)
+    finish(3)
 
     for quarter in range(4):
         landed(mean_ref.at[0, pl.ds(64 * quarter, 64)], r_h.at[0, quarter])
@@ -343,6 +415,8 @@
             pltpu.VMEM((16, 32, 768), f32),
             pltpu.VMEM((256, 768), bf16),
             pltpu.VMEM((4, 8, 128), f32),
+            pltpu.VMEM((3, 64, 768), bf16),
+            pltpu.VMEM((3, 8, 128), f32),
             pltpu.VMEM((16, 32, 768), bf16),
             pltpu.VMEM((4, 8, 64, 768), bf16),
             pltpu.VMEM((4, 8, 8, 128), f32),
@@ -352,6 +426,7 @@
             pltpu.VMEM((8, 4, 32, 768), bf16),
             pltpu.VMEM((4, 8, 64, 768), f32),
             pltpu.VMEM((4, 8, 8, 128), f32),
+            pltpu.VMEM((4, 512, 128), f32),
             pltpu.VMEM((4, 4, 64, 768), bf16),
             pltpu.VMEM((4, 4, 64, 768), bf16),
             pltpu.VMEM((4, 4, 8, 128), f32),
@@ -366,6 +441,7 @@
             pltpu.VMEM((4, 8, 128), f32),
             pltpu.VMEM((4, 8, 128), f32),
             dma((2,)),
+            dma((2, 3)), dma((2, 3)),
             dma((2, 4)), dma((2, 4)),
             dma((2, 3, 4)), dma((2, 3, 4)),
             dma((2, 4)), dma((2, 4)),

time: 118 us -> 91.9 us (0.78)
  Pallas kernels: 114 us -> 88.1 us
    pallas_call x1, Pallas kernels: 114 us -> 88.1 us  [per_device(): pl.pallas_call(kernel, out_shape=(jax.ShapeDtypeStruct((1, 256), f32), ja...]
where the time goes in v2:
time: 91.9 us; the launch traced here: 91.7 us
  Pallas kernels  88.1 us (96%)
  local copies, waits for them, and re-layouts  2.96 us (3%)
    pallas_call x1, Pallas kernels, per_device(): pl.pallas_call(kernel, out_shape=(jax.ShapeDtypeStruct((1, 256), f32), ja...  88.1 us
    unnamed x2, local copies, waits for them, and re-layouts  2.96 us

profile of v2, /device:TPU:4, one launch (start us, length us, event | category | flops | bytes accessed | tf_op | source)
XLA Modules:
  0.0 91.7 jit_solution(3421737361930810775)
XLA Ops:
  0.6 88.1 %dedup_scores.1 = (f32[1,256]{1,0:T(1,128)}, bf16[1,256,768]{2,1,0:T(8,128)(2,1)}) custom-call(f32[1,256,768]{2,1,0:T(8,128)} %member_hbm.1, s32[16]{0:T(128)} %sizes_ref.1, s32[1,256]{1,0:T(1,128)} %order_ref.1, f32[16,32,768]{2,1,0:T(8,128)} %ref_hbm.1), custom_call_target="tpu_custom_call" | custom-call | flops 9663676416 | bytes 4194304 | tf_op jit(solution)/shard_map/dedup_scores/pallas_call | solution.py:408
  88.7 1.2 %copy.8 = f32[1,256]{1,0:T(1,128)} copy(f32[1,256]{1,0:T(1,128)} %get-tuple-element.4) | data formatting | bytes 2048
  89.9 1.8 %copy.9 = bf16[1,256,768]{2,1,0:T(8,128)(2,1)} copy(bf16[1,256,768]{2,1,0:T(8,128)(2,1)} %get-tuple-element.5) | data formatting | bytes 786432

commit v3 on v2

--- a/solution.py
+++ b/solution.py
@@ -11,7 +11,7 @@
 SCALE = 32
 MESH = pl.DeviceIdType.MESH
 LOG2E = math.log2(math.e)
-STEPS = (0, 4, 1, 7, 2, 6, 3, 5)
+STEPS = (0, 2, 6, 1, 7, 3, 5, 4)
 
 
 def unit_rows(values):
@@ -45,7 +45,7 @@
     member_hbm, sizes_ref, order_ref, ref_hbm, log_ref, mean_ref,
     member_in, ref_in, home_rows, home_rank, hop_rows, hop_rank, ref_unit, query, rank, key_member, rank_partner, ref_other, key_ref,
     part_sum, part_total, lane_total, mix_send, mix_recv, tot_send, tot_recv, own_mix, own_tot,
-    x_send, x_recv, xt_send, xt_recv, done_rows, done_log, home_log,
+    x_send, x_recv, xt_send, xt_recv, chain_rows, chain_total, done_rows, done_log, home_log,
     load_sem, s_q, r_q, s_a, r_a, s_x, r_x, s_c, r_c, s_y, r_y, s_z, r_z, s_ry, r_ry,
     s_m, r_m, s_t, r_t, s_h, r_h,
 ):
@@ -282,20 +282,40 @@
         part_total[t, my_half] = total
         x_send[t] = mixed.astype(jnp.bfloat16)
         xt_send[t] = total
-        for i, step in enumerate(x_steps):
-            to_x = (x + step) % 4
-            target = device(to_x, y, z, core)
-            send(x_send.at[t, to_x], x_recv.at[t, i], s_t.at[0, i, t], r_t.at[0, i, t], target)
-            send(xt_send.at[t, to_x], xt_recv.at[t, i], s_t.at[1, i, t], r_t.at[1, i, t], target)
+        if t == 3:
+            for i, step in enumerate(x_steps):
+                send_part(t, i, x_send.at[t, (x + step) % 4], xt_send.at[t, (x + step) % 4], (x + step) % 4)
+        else:
+            far, near = (x + 2) % 4, (x + 4 - onward) % 4
+            send_part(t, 0, x_send.at[t, far], xt_send.at[t, far], (x + onward) % 4)
+            send_part(t, 1, x_send.at[t, near], xt_send.at[t, near], near)
+
+    onward = x_steps[1]
+
+    def send_part(t, i, rows, total, to_x):
+        target = device(to_x, y, z, core)
+        send(rows, x_recv.at[t, i], s_t.at[0, i, t], r_t.at[0, i, t], target)
+        send(total, xt_recv.at[t, i], s_t.at[1, i, t], r_t.at[1, i, t], target)
+
+    def part_landed(t, i):
+        landed(x_recv.at[t, i], r_t.at[0, i, t])
+        landed(xt_recv.at[t, i], r_t.at[1, i, t])
+
+    def add_onward(t):
+        part_landed(t, 0)
+        to_x = (x + onward) % 4
+        owner = core * 4 + to_x
+        chain_rows[t] = (part_sum[t, owner] + x_recv[t, 0].astype(jnp.float32)).astype(jnp.bfloat16)
+        chain_total[t] = part_total[t, owner] + xt_recv[t, 0]
+        send_part(t, 2, chain_rows.at[t], chain_total.at[t], to_x)
 
     last = []
 
     def finish(t):
         mixed = part_sum[t, me]
         total = part_total[t, me]
-        for i in (1, 2, 0):
-            landed(x_recv.at[t, i], r_t.at[0, i, t])
-            landed(xt_recv.at[t, i], r_t.at[1, i, t])
+        for i in (1, 2, 0) if t == 3 else (1, 2):
+            part_landed(t, i)
             mixed = mixed + x_recv[t, i].astype(jnp.float32)
             total = total + xt_recv[t, i]
         from_z = source_z(t)
@@ -326,13 +346,13 @@
             def _():
                 remote.start()
 
+    to_row(3)
     send_refs(1)
+    send_refs(2)
     pass_refs(0)
-    to_row(3)
     to_row(1)
     to_row(2)
     to_row(0)
-    send_refs(2)
     send_refs(3)
     send_refs(4)
     send_refs(5)
@@ -340,26 +360,26 @@
     send_refs(7)
     pass_queries(0)
     pass_refs(1)
+    pass_refs(2)
     pass_queries(1)
     pass_queries(2)
-    pass_refs(2)
     pass_refs(3)
+    pass_refs(4)
     share_queries(0)
     pass_queries(3)
-    pass_refs(4)
-    pass_refs(5)
     share_queries(1)
     share_queries(2)
+    pass_refs(5)
+    pass_refs(6)
     queries_landed(0)
     refs_landed(0)
     compute_refs(0, 0)
     queries_landed(1)
     compute_refs(1, 0)
-    pass_refs(6)
+    share_queries(3)
+    pass_refs(7)
     queries_landed(2)
     compute_refs(2, 0)
-    pass_refs(7)
-    share_queries(3)
     members_landed()
     compute_members(0)
     compute_members(1)
@@ -380,6 +400,9 @@
     to_sibling(3)
     to_owner(2)
     to_owner(3)
+    add_onward(0)
+    add_onward(1)
+    add_onward(2)
     finish(0)
     finish(1)
     finish(2)
@@ -400,12 +423,17 @@
             remote.wait_send()
 
 
+def hand_out(log_in, mean_in, log_out, mean_out):
+    log_out[...] = log_in[...]
+    mean_out[...] = mean_in[...]
+
+
 def per_device(member_embed, sizes, order, ref_embed):
     vmem = pl.BlockSpec(memory_space=pltpu.VMEM)
     anywhere = pl.BlockSpec(memory_space=pl.ANY)
     bf16, f32 = jnp.bfloat16, jnp.float32
     dma = pltpu.SemaphoreType.DMA
-    return pl.pallas_call(
+    log_total, neighbour = pl.pallas_call(
         kernel,
         out_shape=(jax.ShapeDtypeStruct((1, 256), f32), jax.ShapeDtypeStruct((1, 256, 768), bf16)),
         in_specs=[anywhere, pl.BlockSpec(memory_space=pltpu.SMEM), vmem, anywhere],
@@ -437,6 +465,8 @@
             pltpu.VMEM((4, 3, 64, 768), bf16),
             pltpu.VMEM((4, 4, 8, 128), f32),
             pltpu.VMEM((4, 3, 8, 128), f32),
+            pltpu.VMEM((3, 64, 768), bf16),
+            pltpu.VMEM((3, 8, 128), f32),
             pltpu.VMEM((4, 64, 768), bf16),
             pltpu.VMEM((4, 8, 128), f32),
             pltpu.VMEM((4, 8, 128), f32),
@@ -458,6 +488,14 @@
         cost_estimate=pl.CostEstimate(flops=4 * 2048 * 1536 * 768, bytes_accessed=4 << 20, transcendentals=2048 * 1536),
         name="dedup_scores",
     )(member_embed, sizes, order, ref_embed)
+    return pl.pallas_call(
+        hand_out,
+        out_shape=(jax.ShapeDtypeStruct((1, 256), f32), jax.ShapeDtypeStruct((1, 256, 768), bf16)),
+        in_specs=[vmem, vmem],
+        out_specs=(vmem, vmem),
+        cost_estimate=pl.CostEstimate(flops=0, bytes_accessed=1 << 20, transcendentals=0),
+        name="hand_out",
+    )(log_total, neighbour)
 
 
 def solution(mesh):

time: 91.9 us -> 88.9 us (0.967)
  the two profiles are of different devices: /device:TPU:4 before, /device:TPU:3 now
where the time goes in v3:
time: 88.9 us; the launch traced here: 88.8 us
  Pallas kernels  88.1 us (99%)
    pallas_call x1, Pallas kernels, per_device(): pl.pallas_call(kernel, out_shape=(jax.ShapeDtypeStruct((1, 256), f32), ja...  86.4 us

profile of v3, /device:TPU:3, one launch (start us, length us, event | category | flops | bytes accessed | tf_op | source)
XLA Modules:
  0.0 88.8 jit_solution(11360241833428104405)
XLA Ops:
  0.6 86.4 %dedup_scores.1 = (f32[1,256]{1,0:T(1,128)}, bf16[1,256,768]{2,1,0:T(8,128)(2,1)}) custom-call(f32[1,256,768]{2,1,0:T(8,128)} %member_hbm.1, s32[16]{0:T(128)} %sizes_ref.1, s32[1,256]{1,0:T(1,128)} %order_ref.1, f32[16,32,768]{2,1,0:T(8,128)} %ref_hbm.1), custom_call_target="tpu_custom_call" | custom-call | flops 9663676416 | bytes 4194304 | tf_op jit(solution)/shard_map/dedup_scores/pallas_call | solution.py:436
  87.0 1.8 %hand_out.1 = (f32[1,256]{1,0:T(1,128)}, bf16[1,256,768]{2,1,0:T(8,128)(2,1)}) custom-call(f32[1,256]{1,0:T(1,128)} %get-tuple-element.4.log_in, bf16[1,256,768]{2,1,0:T(8,128)(2,1)} %get-tuple-element.5.mean_in), custom_call_target="tpu_custom_call" | custom-call | bytes 1048576 | tf_op jit(solution)/shard_map/hand_out/pallas_call | solution.py:491

commit v4 on v3

--- a/solution.py
+++ b/solution.py
@@ -218,19 +218,17 @@
             landed(key_member.at[1, t], r_y.at[0, t])
             landed(rank_partner.at[t], r_y.at[1, t])
 
-    def refs_landed(half):
-        for i in range(4 * half, 4 * half + 4):
+    def refs_landed(first, last):
+        for i in range(first, last):
             for side in range(3):
                 landed(key_ref.at[i, side + 1], r_ry.at[side, i])
 
-    def weigh(t, keys):
-        logits = lax.dot_general(
-            query[t].reshape(512, 768), keys, (((1,), (1,)), ((), ())), preferred_element_type=jnp.float32
-        )
+    def weigh(rows, keys):
+        logits = lax.dot_general(rows, keys, (((1,), (1,)), ((), ())), preferred_element_type=jnp.float32)
         return jnp.exp2(logits * (SCALE / 768 * LOG2E) - SCALE * LOG2E)
 
     def lane_sums(weight):
-        return weight[:, 0:128] + weight[:, 128:256] + weight[:, 256:384] + weight[:, 384:512]
+        return sum(weight[:, at : at + 128] for at in range(128, weight.shape[1], 128)) + weight[:, 0:128]
 
     begun = set()
 
@@ -256,22 +254,32 @@
         )[0:1]
         row_rank = jnp.concatenate([lanes_to_rows(rank[t, owner]) for owner in range(8)], axis=0)
         keys = key_member[...].reshape(512, 768)
-        weight = jnp.where(key_rank < row_rank, weigh(t, keys), 0.0)
+        weight = jnp.where(key_rank < row_rank, weigh(query[t].reshape(512, 768), keys), 0.0)
         add_up(t, weight, keys)
 
-    def compute_refs(t, half):
-        keys = key_ref[pl.ds(4 * half, 4)].reshape(512, 768)
-        weight = weigh(t, keys)
-        add_up(t, weight, keys)
-
-    def to_sibling(t):
-        total = jnp.sum(lane_total[t], axis=1, keepdims=True)
-        for owner in range(8):
-            part_total[t, owner] = rows_to_lanes(total[64 * owner : 64 * owner + 64])
-        mix_send[t] = part_sum[t, other_half].astype(jnp.bfloat16)
-        tot_send[t] = part_total[t, other_half]
-        send(mix_send.at[t], mix_recv.at[t], s_m.at[0, t], r_m.at[0, t], sibling)
-        send(tot_send.at[t], tot_recv.at[t], s_m.at[1, t], r_m.at[1, t], sibling)
+    def compute_refs(t, first, last):
+        keys = key_ref[pl.ds(first, last - first)].reshape((last - first) * 128, 768)
+        add_up(t, weigh(query[t].reshape(512, 768), keys), keys)
+
+    def compute_last(t):
+        keys = key_ref[pl.ds(4, 4)].reshape(512, 768)
+        for side in (other, core):
+            part = pl.ds(side * 4, 4)
+            weight = weigh(query[t, part].reshape(256, 768), keys)
+            sums = lane_total[t, pl.ds(pl.multiple_of(side * 256, 256), 256)] + lane_sums(weight)
+            total = jnp.sum(sums, axis=1, keepdims=True)
+            mixed = jnp.dot(weight.astype(jnp.bfloat16), keys, preferred_element_type=jnp.float32)
+            mixed = part_sum[t, part] + mixed.reshape(4, 64, 768)
+            if side is other:
+                for owner in range(4):
+                    tot_send[t, owner] = rows_to_lanes(total[64 * owner : 64 * owner + 64])
+                mix_send[t] = mixed.astype(jnp.bfloat16)
+                send(mix_send.at[t], mix_recv.at[t], s_m.at[0, t], r_m.at[0, t], sibling)
+                send(tot_send.at[t], tot_recv.at[t], s_m.at[1, t], r_m.at[1, t], sibling)
+            else:
+                for owner in range(4):
+                    part_total[t, side * 4 + owner] = rows_to_lanes(total[64 * owner : 64 * owner + 64])
+                part_sum[t, part] = mixed
 
     def to_owner(t):
         landed(mix_recv.at[t], r_m.at[0, t])
@@ -372,32 +380,28 @@
     pass_refs(5)
     pass_refs(6)
     queries_landed(0)
-    refs_landed(0)
-    compute_refs(0, 0)
+    refs_landed(0, 4)
+    compute_refs(0, 0, 4)
     queries_landed(1)
-    compute_refs(1, 0)
+    compute_refs(1, 0, 4)
     share_queries(3)
     pass_refs(7)
     queries_landed(2)
-    compute_refs(2, 0)
+    compute_refs(2, 0, 4)
     members_landed()
     compute_members(0)
     compute_members(1)
+    queries_landed(3)
+    compute_refs(3, 0, 4)
+    refs_landed(4, 8)
+    compute_last(0)
+    compute_last(1)
+    to_owner(0)
     compute_members(2)
-    queries_landed(3)
-    compute_refs(3, 0)
+    compute_last(2)
+    to_owner(1)
     compute_members(3)
-    refs_landed(1)
-    compute_refs(0, 1)
-    to_sibling(0)
-    compute_refs(1, 1)
-    to_sibling(1)
-    to_owner(0)
-    compute_refs(2, 1)
-    to_sibling(2)
-    to_owner(1)
-    compute_refs(3, 1)
-    to_sibling(3)
+    compute_last(3)
     to_owner(2)
     to_owner(3)
     add_onward(0)

time: 88.9 us -> 86.9 us (0.978)
  the two profiles are of different devices: /device:TPU:3 before, /device:TPU:4 now
where the time goes in v4:
time: 86.9 us; the launch traced here: 85.5 us
  Pallas kernels  84.8 us (98%)
    pallas_call x1, Pallas kernels, per_device(): pl.pallas_call(kernel, out_shape=(jax.ShapeDtypeStruct((1, 256), f32), ja...  83.1 us
    pallas_call x1, Pallas kernels, per_device(): pl.pallas_call(hand_out, out_shape=(jax.ShapeDtypeStruct((1, 256), f32),...  1.77 us

profile of v4, /device:TPU:4, one launch (start us, length us, event | category | flops | bytes accessed | tf_op | source)
XLA Modules:
  0.0 85.5 jit_solution(10720337263675394750)
XLA Ops:
  0.6 83.1 %dedup_scores.1 = (f32[1,256]{1,0:T(1,128)}, bf16[1,256,768]{2,1,0:T(8,128)(2,1)}) custom-call(f32[1,256,768]{2,1,0:T(8,128)} %member_hbm.1, s32[16]{0:T(128)} %sizes_ref.1, s32[1,256]{1,0:T(1,128)} %order_ref.1, f32[16,32,768]{2,1,0:T(8,128)} %ref_hbm.1), custom_call_target="tpu_custom_call" | custom-call | flops 9663676416 | bytes 4194304 | tf_op jit(solution)/shard_map/dedup_scores/pallas_call | solution.py:440
  83.7 1.8 %hand_out.1 = (f32[1,256]{1,0:T(1,128)}, bf16[1,256,768]{2,1,0:T(8,128)(2,1)}) custom-call(f32[1,256]{1,0:T(1,128)} %get-tuple-element.4.log_in, bf16[1,256,768]{2,1,0:T(8,128)(2,1)} %get-tuple-element.5.mean_in), custom_call_target="tpu_custom_call" | custom-call | bytes 1048576 | tf_op jit(solution)/shard_map/hand_out/pallas_call | solution.py:495

commit v5 on v4

--- a/solution.py
+++ b/solution.py
@@ -391,8 +391,6 @@
     members_landed()
     compute_members(0)
     compute_members(1)
-    queries_landed(3)
-    compute_refs(3, 0, 4)
     refs_landed(4, 8)
     compute_last(0)
     compute_last(1)
@@ -400,6 +398,8 @@
     compute_members(2)
     compute_last(2)
     to_owner(1)
+    queries_landed(3)
+    compute_refs(3, 0, 4)
     compute_members(3)
     compute_last(3)
     to_owner(2)

time: 86.9 us -> 86.2 us (level); the launches traced: 85.5 us -> 86 us
  no operation moved by 1% of the time
where the time goes in v5:
time: 86.2 us; the launch traced here: 86 us
  Pallas kernels  85.4 us (99%)
    pallas_call x1, Pallas kernels, per_device(): pl.pallas_call(kernel, out_shape=(jax.ShapeDtypeStruct((1, 256), f32), ja...  83.6 us
    pallas_call x1, Pallas kernels, per_device(): pl.pallas_call(hand_out, out_shape=(jax.ShapeDtypeStruct((1, 256), f32),...  1.77 us

profile of v5, /device:TPU:4, one launch (start us, length us, event | category | flops | bytes accessed | tf_op | source)
XLA Modules:
  0.0 86.0 jit_solution(8117786254416714624)
XLA Ops:
  0.6 83.6 %dedup_scores.1 = (f32[1,256]{1,0:T(1,128)}, bf16[1,256,768]{2,1,0:T(8,128)(2,1)}) custom-call(f32[1,256,768]{2,1,0:T(8,128)} %member_hbm.1, s32[16]{0:T(128)} %sizes_ref.1, s32[1,256]{1,0:T(1,128)} %order_ref.1, f32[16,32,768]{2,1,0:T(8,128)} %ref_hbm.1), custom_call_target="tpu_custom_call" | custom-call | flops 9663676416 | bytes 4194304 | tf_op jit(solution)/shard_map/dedup_scores/pallas_call | solution.py:440
  84.3 1.8 %hand_out.1 = (f32[1,256]{1,0:T(1,128)}, bf16[1,256,768]{2,1,0:T(8,128)(2,1)}) custom-call(f32[1,256]{1,0:T(1,128)} %get-tuple-element.4.log_in, bf16[1,256,768]{2,1,0:T(8,128)(2,1)} %get-tuple-element.5.mean_in), custom_call_target="tpu_custom_call" | custom-call | bytes 1048576 | tf_op jit(solution)/shard_map/hand_out/pallas_call | solution.py:495
